TPU v7x, 32 devices: a whole 2x2x4 slice. The times are simulated.
32 devices in a mesh: groups: 1, row: 32 (over z, y, x, core).
Axes of the slice: x: 2, y: 2, z: 4, core: 2. Of those that a mesh axis runs over, the one named last changes fastest.
Arguments:
- pair: float32 [384, 384, 128], P(('groups', 'row')), may hold values from -6 to 6
- mask: int32 [384], P('groups'), may hold values from 0 to 1, as said below
- tri_in: bfloat16 [128, 512], replicated, may hold values from -0.5 to 0.5
- tri_gate: bfloat16 [128, 128], replicated, may hold values from -0.5 to 0.5
- tri_out: bfloat16 [128, 128], replicated, may hold values from -0.5 to 0.5
- att_in: bfloat16 [128, 512], replicated
- att_bias: bfloat16 [128, 4], replicated, may hold values from -0.5 to 0.5
- att_out: bfloat16 [128, 128], replicated, may hold values from -0.5 to 0.5
Outputs:
- updated: float32 [384, 384, 128], P(('groups', 'row'))
Inputs may be any that keep to these rules, and one draw needn't show every extreme that they name: mask is 1 on the first L residues and 0 on the rest, with 192 <= L < 384.
All inputs are finite; a program needn't handle non-finite values.
Results may differ from a plain program's by a relative error of at most 0.0075.
Values may be sent and summed in bfloat16 or wider, within the bound.
A program may use at most 192 MiB of HBM per device.

v0:
```python
import jax
import jax.numpy as jnp
from jax import lax
from jax.sharding import PartitionSpec as P


def layer_norm(value):
    center = value - jnp.mean(value, axis=-1, keepdims=True)
    return center / jnp.sqrt(jnp.mean(center * center, axis=-1, keepdims=True) + 1e-05)


def per_device(pair, mask, tri_in, tri_gate, tri_out, att_in, att_bias, att_out):
    own_rows = pair.shape[0]
    residues = pair.shape[1]
    width = pair.shape[2]
    heads = att_bias.shape[1]
    head_size = att_out.shape[0] // heads
    valid = mask.astype(jnp.float32)
    start_row = lax.axis_index("row") * own_rows
    row_valid = lax.dynamic_slice_in_dim(valid, start_row, own_rows, 0)
    pair_mask = row_valid[:, None] * valid[None, :]
    normed = layer_norm(pair).astype(jnp.bfloat16)
    proj = jnp.einsum("rkc,cf->rkf", normed, tri_in, preferred_element_type=jnp.float32)
    left = (
        jax.nn.sigmoid(proj[..., width : 2 * width]) * proj[..., :width] * pair_mask[..., None]
    ).astype(jnp.bfloat16)
    right = (
        jax.nn.sigmoid(proj[..., 3 * width :])
        * proj[..., 2 * width : 3 * width]
        * pair_mask[..., None]
    ).astype(jnp.bfloat16)
    left_by_channel = jnp.transpose(left, (2, 0, 1))
    right_by_channel = jnp.transpose(right, (2, 0, 1))
    left_all, right_all = (
        lax.all_to_all(left_by_channel, "row", split_axis=0, concat_axis=1, tiled=True),
        lax.all_to_all(right_by_channel, "row", split_axis=0, concat_axis=1, tiled=True),
    )
    tri_channel = jnp.einsum(
        "cik,cjk->cij", left_all, right_all, preferred_element_type=jnp.float32
    )
    tri_rows = lax.all_to_all(
        tri_channel.astype(jnp.bfloat16), "row", split_axis=1, concat_axis=0, tiled=True
    ).astype(tri_channel.dtype)
    tri = jnp.transpose(tri_rows, (1, 2, 0))
    tnorm = layer_norm(tri).astype(jnp.bfloat16)
    update = jnp.einsum("rkc,cf->rkf", tnorm, tri_out, preferred_element_type=jnp.float32)
    gating = jax.nn.sigmoid(
        jnp.einsum("rkc,cf->rkf", normed, tri_gate, preferred_element_type=jnp.float32)
    )
    pair1 = pair + pair_mask[..., None] * gating * update
    ynorm = layer_norm(pair1).astype(jnp.bfloat16)
    qkvg = jnp.einsum("rkc,cf->rkf", ynorm, att_in, preferred_element_type=jnp.float32)
    qkvg = qkvg.reshape(own_rows, residues, 4, heads, head_size)
    query = qkvg[:, :, 0].astype(jnp.bfloat16)
    keys = qkvg[:, :, 1].astype(jnp.bfloat16)
    values = qkvg[:, :, 2].astype(jnp.bfloat16)
    gates = qkvg[:, :, 3]
    local_bias = jnp.einsum(
        "rkc,ch->hrk", ynorm, att_bias, preferred_element_type=jnp.float32
    ).astype(jnp.bfloat16)
    bias = lax.all_gather(local_bias, "row", axis=1, tiled=True)
    scores = jnp.einsum(
        "ijhd,ikhd->ihjk", query, keys, preferred_element_type=jnp.float32
    ) / jnp.sqrt(jnp.float32(head_size))
    scores = scores + bias.astype(jnp.float32)[None]
    scores = jnp.where(mask[None, None, None, :] > 0, scores, jnp.float32(-1000000000.0))
    probs = jax.nn.softmax(scores, axis=-1).astype(jnp.bfloat16)
    mixed = jnp.einsum("ihjk,ikhd->ijhd", probs, values, preferred_element_type=jnp.float32)
    att = (
        (jax.nn.sigmoid(gates) * mixed)
        .astype(jnp.bfloat16)
        .reshape(own_rows, residues, heads * head_size)
    )
    out = jnp.einsum("rkf,fc->rkc", att, att_out, preferred_element_type=jnp.float32)
    return pair1 + row_valid[:, None, None] * out


def solution(mesh):
    return jax.shard_map(
        per_device,
        mesh=mesh,
        in_specs=(P(("groups", "row"), None, None), P("groups"), P(), P(), P(), P(), P(), P()),
        out_specs=P(("groups", "row"), None, None),
        check_vma=False,
    )
```

profile of v0, /device:TPU:0, one launch (start us, length us, event | category | flops | bytes accessed | tf_op | source)
XLA Modules:
  0.0 264.8 jit_solution(11438715121588632043)
XLA Ops:
  7.5 2.3 reduce_sum.63
  11.4 3.9 %fusion.34 = f32[12,384,512]{1,2,0:T(8,128)S(1)} fusion(bf16[128,512]{1,0:T(8,128)(2,1)S(1)} %copy-done, f32[12,384,128]{2,1,0:T(8,128)S(1)} %copy-done.2, f32[12,384]{1,0:T(8,128)S(1)} %add_sqrt_fusion.2, f32[12,384]{1,0:T(8,128)S(1)} %broadcast_multiply_fusion.2), kind=kOutput, calls=%fused_computation.58 | convolution fusion | flops 605749248 | bytes 11964416 | tf_op jit(solution)/shard_map/rkc,cf->rkf/dot_general | solution.py:23
  15.3 2.2 fusion.28
  19.4 7.4 %all-to-all-start = ((bf16[128,12,384]{2,1,0:T(8,128)(2,1)}), bf16[128,12,384]{2,1,0:T(8,128)(2,1)}, u32[]{:S(2)}, u32[]{:S(2)}) async-start(bf16[128,12,384]{2,1,0:T(8,128)(2,1)} %copy.81), calls=%async_computation | async-start | bytes 3145728 | tf_op jit(solution)/shard_map/all_to_all | solution.py:35
  26.8 3.1 %copy.85 = bf16[128,12,384]{2,1,0:T(8,128)(2,1)} copy(bf16[128,12,384]{2,0,1:T(8,128)(2,1)} %get-tuple-element.6) | data formatting | bytes 2359296 | tf_op jit(solution)/shard_map/transpose | solution.py:33
  30.0 34.6 %all-to-all-done = bf16[128,12,384]{2,1,0:T(8,128)(2,1)} async-done(((bf16[128,12,384]{2,1,0:T(8,128)(2,1)}), bf16[128,12,384]{2,1,0:T(8,128)(2,1)}, u32[]{:S(2)}, u32[]{:S(2)}) %all-to-all-start) | async-done | bytes 1179680 | tf_op jit(solution)/shard_map/all_to_all | solution.py:35
  64.6 3.9 %all-to-all-start.1 = ((bf16[128,12,384]{2,1,0:T(8,128)(2,1)}), bf16[128,12,384]{2,1,0:T(8,128)(2,1)}, u32[]{:S(2)}, u32[]{:S(2)}) async-start(bf16[128,12,384]{2,1,0:T(8,128)(2,1)} %copy.85), calls=%async_computation.1 | async-start | bytes 3145728 | tf_op jit(solution)/shard_map/all_to_all | solution.py:36
  68.4 2.9 %copy.82 = bf16[32,4,12,384]{3,1,2,0:T(4,128)(2,1)} copy(bf16[32,4,12,384]{3,2,1,0:T(8,128)(2,1)} %bitcast.3) | data formatting | bytes 2359296 | tf_op jit(solution)/shard_map/all_to_all | solution.py:35
  71.3 34.8 %all-to-all-done.1 = bf16[128,12,384]{2,1,0:T(8,128)(2,1)} async-done(((bf16[128,12,384]{2,1,0:T(8,128)(2,1)}), bf16[128,12,384]{2,1,0:T(8,128)(2,1)}, u32[]{:S(2)}, u32[]{:S(2)}) %all-to-all-start.1) | async-done | bytes 1179680 | tf_op jit(solution)/shard_map/all_to_all | solution.py:36
  106.2 2.0 copy.86
  111.0 3.9 %all-to-all-start.2 = ((bf16[4,384,384]{2,0,1:T(4,128)(2,1)}), bf16[4,384,384]{2,0,1:T(4,128)(2,1)}, u32[]{:S(2)}, u32[]{:S(2)}) async-start(bf16[4,384,384]{2,0,1:T(4,128)(2,1)} %copy.89), calls=%async_computation.2 | async-start | bytes 2359296 | tf_op jit(solution)/shard_map/all_to_all | solution.py:41
  117.1 3.3 %fusion.38 = f32[12,384,128]{1,2,0:T(8,128)} fusion(bf16[128,128]{1,0:T(8,128)(2,1)S(1)} %copy-done.11, f32[12,384,128]{2,1,0:T(8,128)S(1)} %copy-done.2, f32[12,384]{1,0:T(8,128)S(1)} %add_sqrt_fusion.2, f32[12,384]{1,0:T(8,128)S(1)} %broadcast_multiply_fusion.2), kind=kOutput, calls=%fused_computation.62 | convolution fusion | flops 152764416 | bytes 4788224 | tf_op jit(solution)/shard_map/rkc,cf->rkf/dot_general | solution.py:48
  120.5 23.5 %all-to-all-done.2 = bf16[4,384,384]{2,0,1:T(4,128)(2,1)} async-done(((bf16[4,384,384]{2,0,1:T(4,128)(2,1)}), bf16[4,384,384]{2,0,1:T(4,128)(2,1)}, u32[]{:S(2)}, u32[]{:S(2)}) %all-to-all-start.2) | async-done | bytes 1179680 | tf_op jit(solution)/shard_map/all_to_all | solution.py:41
  145.6 2.0 copy.90
  147.5 2.7 %reshape.90 = f32[128,12,384]{2,0,1:T(8,128)S(1)} reshape(f32[32,4,12,384]{3,1,0,2:T(4,128)} %copy.90) | data formatting | bytes 4718592 | tf_op jit(solution)/shard_map/transpose | solution.py:44
  153.5 2.8 %fusion.43 = (f32[12,384]{1,0:T(8,128)S(1)}, f32[12,384,128]{1,2,0:T(8,128)S(1)}) fusion(f32[12,384,128]{1,2,0:T(8,128)S(1)} %copy-done.5, bf16[128,128]{1,0:T(8,128)(2,1)S(1)} %copy-done.12, f32[128,12,384]{2,0,1:T(8,128)} %copy-done.3, f32[12,384]{1,0:T(8,128)S(1)} %add_sqrt_fusion.1, f32[12,384]{1,0:T(8,128)S(1)} %broadcast_multiply_fusion.1, ...), kind=kOutput, calls=%fused_computation.76 | convolution fusion | flops 156888576 | bytes 9543680 | tf_op jit(solution)/shard_map/rkc,cf->rkf/dot_general | solution.py:46
  158.9 6.3 %fusion.32 = f32[12,384,512]{1,2,0:T(8,128)} fusion(bf16[12,384,128]{1,2,0:T(8,128)(2,1)} %copy-done.4, bf16[128,512]{1,0:T(8,128)(2,1)S(1)} %copy-done.7), kind=kOutput, calls=%fused_computation.56 | convolution fusion | flops 603979776 | bytes 10747904 | tf_op jit(solution)/shard_map/rkc,cf->rkf/dot_general | solution.py:52
  165.2 46.9 %all-gather.2.cloned.1.call-done = bf16[4,384,384]{2,0,1:T(4,128)(2,1)} async-done(((bf16[4,12,384]{2,0,1:T(4,128)(2,1)}), bf16[4,384,384]{2,0,1:T(4,128)(2,1)}) %all-gather.2.cloned.1.call-update) | async-done | bytes 1179664 | tf_op jit(solution)/shard_map/all_gather | solution.py:61
  212.1 2.8 %copy_convert_fusion = f32[4,384,384]{2,1,0:T(8,128)} fusion(bf16[4,384,384]{2,0,1:T(4,128)(2,1)} %all-gather.2.cloned.1.call-done), kind=kLoop, calls=%fused_computation.47 | loop fusion | flops 589824 | bytes 3538944 | tf_op jit(solution)/shard_map/convert_element_type | solution.py:65
  214.9 3.0 %copy.100 = f32[4,384,384]{1,2,0:T(8,128)} copy(f32[4,384,384]{2,1,0:T(8,128)} %copy_convert_fusion) | data formatting | bytes 4718592 | tf_op jit(solution)/shard_map/convert_element_type | solution.py:65
  217.9 20.1 %fusion.44 = (f32[12,4,384]{2,1,0:T(4,128)S(1)}, f32[12,4,384,384]{2,3,1,0:T(8,128)}) fusion(f32[4,384,384]{1,2,0:T(8,128)} %copy.100, pred[384]{0:T(512)(128)(4,1)S(1)} %broadcast_compare_fusion, f32[12,384,4,4,32]{1,4,3,2,0:T(8,128)} %bitcast.90), kind=kOutput, calls=%fused_computation.77 | convolution fusion | flops 488374656 | bytes 33104256 | tf_op jit(solution)/shard_map/sub | solution.py:67
  238.0 13.6 %fusion.24 = bf16[12,384,4,32]{1,3,2,0:T(8,128)(2,1)} fusion(f32[12,4,384,384]{2,3,1,0:T(8,128)} %get-tuple-element.10, f32[12,4,384]{2,1,0:T(4,128)S(1)} %get-tuple-element.9, f32[12,384,4,4,32]{1,4,3,2,0:T(8,128)} %bitcast.91), kind=kOutput, calls=%fused_computation.42 | convolution fusion | flops 470089728 | bytes 33103872 | tf_op jit(solution)/shard_map/ihjk,ikhd->ijhd/dot_general | solution.py:68
  251.7 3.2 %multiply_add_fusion = f32[12,384,128]{1,2,0:T(8,128)} fusion(f32[12,384,128]{1,2,0:T(8,128)S(1)} %get-tuple-element.8, bf16[12,384,128]{1,2,0:T(8,128)(2,1)} %bitcast.93, f32[12]{0:T(128)S(1)} %dynamic_slice.3, bf16[128,128]{1,0:T(8,128)(2,1)S(1)} %copy-done.8), kind=kOutput, calls=%fused_computation.34 | convolution fusion | flops 152174592 | bytes 5931056 | tf_op jit(solution)/shard_map/rkf,fc->rkc/dot_general | solution.py:74
  254.9 3.0 %copy.104 = f32[12,384,128]{2,1,0:T(8,128)} copy(f32[12,384,128]{1,2,0:T(8,128)} %multiply_add_fusion) | data formatting | bytes 4718592 | tf_op jit(solution)/shard_map/add | solution.py:75
  (51 shorter events, 16.7 us)
Async XLA Ops:
  6.5 4.8 %copy-start = (bf16[128,512]{1,0:T(8,128)(2,1)S(1)}, bf16[128,512]{1,0:T(8,128)(2,1)}, u32[]{:S(2)}) copy-start(bf16[128,512]{1,0:T(8,128)(2,1)} %param.10) | copy-start | bytes 393220
  6.5 3.4 %copy-start.2 = (f32[12,384,128]{2,1,0:T(8,128)S(1)}, f32[12,384,128]{2,1,0:T(8,128)}, u32[]{:S(2)}) copy-start(f32[12,384,128]{2,1,0:T(8,128)} %param.8) | copy-start | bytes 7077892
  19.4 45.1 %all-to-all-start = ((bf16[128,12,384]{2,1,0:T(8,128)(2,1)}), bf16[128,12,384]{2,1,0:T(8,128)(2,1)}, u32[]{:S(2)}, u32[]{:S(2)}) async-start(bf16[128,12,384]{2,1,0:T(8,128)(2,1)} %copy.81), calls=%async_computation | async-start | bytes 3145728 | tf_op jit(solution)/shard_map/all_to_all | solution.py:35
  64.6 41.6 %all-to-all-start.1 = ((bf16[128,12,384]{2,1,0:T(8,128)(2,1)}), bf16[128,12,384]{2,1,0:T(8,128)(2,1)}, u32[]{:S(2)}, u32[]{:S(2)}) async-start(bf16[128,12,384]{2,1,0:T(8,128)(2,1)} %copy.85), calls=%async_computation.1 | async-start | bytes 3145728 | tf_op jit(solution)/shard_map/all_to_all | solution.py:36
  106.2 2.0 copy-start.6
  111.0 33.0 %all-to-all-start.2 = ((bf16[4,384,384]{2,0,1:T(4,128)(2,1)}), bf16[4,384,384]{2,0,1:T(4,128)(2,1)}, u32[]{:S(2)}, u32[]{:S(2)}) async-start(bf16[4,384,384]{2,0,1:T(4,128)(2,1)} %copy.89), calls=%async_computation.2 | async-start | bytes 2359296 | tf_op jit(solution)/shard_map/all_to_all | solution.py:41
  114.9 2.2 copy-start.11
  114.9 97.1 %all-gather.2.cloned.1.call-start = ((), (), s32[]{:S(2)}) async-start(), calls=%async_computation.3 | async-start | bytes 1216512 | tf_op jit(solution)/shard_map/all_gather | solution.py:61
  150.2 1.4 copy-start.3
  150.2 2.5 copy-start.5
  150.2 2.5 copy-start.12
  150.2 3.2 %copy-start.13 = (f32[12,384,128]{1,2,0:T(8,128)S(1)}, f32[12,384,128]{1,2,0:T(8,128)}, u32[]{:S(2)}) copy-start(f32[12,384,128]{1,2,0:T(8,128)} %fusion.38) | copy-start | bytes 7077892
  156.6 1.4 copy-start.10
  156.6 2.2 copy-start.9
  156.6 2.3 copy-start.7
  156.9 1.0 copy-start.4
  238.0 13.7 %copy-start.8 = (bf16[128,128]{1,0:T(8,128)(2,1)S(1)}, bf16[128,128]{1,0:T(8,128)(2,1)}, u32[]{:S(2)}) copy-start(bf16[128,128]{1,0:T(8,128)(2,1)} %param.15) | copy-start | bytes 98308
  251.7 6.3 %copy-start.1 = (bf16[128,512]{1,0:T(8,128)(2,1)S(1)}, bf16[128,512]{1,0:T(8,128)(2,1)}, u32[]{:S(2)}) copy-start(bf16[128,512]{1,0:T(8,128)(2,1)} %param.10) | copy-start | bytes 393220
Sparse Core Ops, SparseCore 0:
  158.9 53.0 all-gather.1
where the time goes:
time: 266 us; the launch traced here: 265 us
  waiting for transfers between devices  140 us (53%)
  matrix products  55.2 us (21%)
  local copies, waits for them, and re-layouts  28.4 us (11%)
  starting transfers between devices  15.4 us (6%)
  between operations  13.7 us (5%)
  other arithmetic  12.3 us (5%)
    all_gather x1, waiting for transfers between devices, per_device(): bias = lax.all_gather(local_bias, 'row', axis=1, tiled=True)  46.9 us
    all_to_all x1, waiting for transfers between devices, per_device(): lax.all_to_all(right_by_channel, 'row', split_axis=0, concat_axis=1, tile...  34.8 us
    all_to_all x1, waiting for transfers between devices, per_device(): lax.all_to_all(left_by_channel, 'row', split_axis=0, concat_axis=1, tiled...  34.6 us
    all_to_all x1, waiting for transfers between devices, per_device(): lax.all_to_all(tri_channel.astype(jnp.bfloat16), 'row', split_axis=1, con...  23.5 us
    sub x1, matrix products, per_device(): probs = jax.nn.softmax(scores, axis=-1).astype(jnp.bfloat16)  20.1 us
    dot_general x1, matrix products, per_device(): jnp.einsum('ihjk,ikhd->ijhd', probs, values, preferred_element_type=jnp.f...  13.6 us
    all_to_all x1, starting transfers between devices, per_device(): lax.all_to_all(left_by_channel, 'row', split_axis=0, concat_axis=1, tiled...  7.4 us
    dot_general x1, matrix products, per_device(): jnp.einsum('rkc,cf->rkf', ynorm, att_in, preferred_element_type=jnp.float32)  6.34 us
  transfers between devices with their start and end apart: 4, of which 4 were waited for; matrix products, arithmetic and copies ran while one was open for 7% of the time, Pallas kernels for 0%

commit v1 on v0

--- a/solution.py
+++ b/solution.py
@@ -1,7 +1,320 @@
+import functools
+import math
+
 import jax
 import jax.numpy as jnp
 from jax import lax
+from jax.experimental import pallas as pl
+from jax.experimental.pallas import tpu as pltpu
 from jax.sharding import PartitionSpec as P
+
+EPS = 1e-05
+LOG2E = math.log2(math.e)
+MESH = pl.DeviceIdType.MESH
+PLANE = 8
+
+
+def sigmoid(value):
+    return 0.5 * jnp.tanh(0.5 * value) + 0.5
+
+
+def norm_rows(value):
+    center = value - jnp.mean(value, axis=0, keepdims=True)
+    return center * lax.rsqrt(jnp.mean(center * center, axis=0, keepdims=True) + EPS)
+
+
+def scatter_rows(ref, first, stride, value):
+    for q in range(ref.shape[0]):
+        ref[q, pl.ds(first, value.shape[0], stride=stride), :] = value[:, q * 128 : (q + 1) * 128]
+
+
+def gather_rows(ref, first, count, stride):
+    parts = [ref[q, pl.ds(first, count, stride=stride), :] for q in range(ref.shape[0])]
+    return jnp.concatenate(parts, axis=1)
+
+
+def all_rows(ref):
+    return jnp.concatenate([ref[q] for q in range(ref.shape[0])], axis=1)
+
+
+def matmul(a, b):
+    return jnp.dot(a, b, preferred_element_type=jnp.float32)
+
+
+def triangle_kernel(
+    n, pair_ref, pm_ref, tri_in_ref, gate_ref, tri_out_ref, bias_w_ref,
+    pair1_ref, yn_ref, bias_ref,
+    wide, square, xn, left_send, right_send, left_got, right_got, left_mat, tri_send, tri_got, bias_all, bias_wide,
+    left_ssem, left_rsem, right_ssem, right_rsem, tri_ssem, tri_rsem,
+    z_ssem, plane_ssem, core_ssem, bias_rsem,
+):
+    rows, residues, width = pair_ref.shape
+    per = width // n
+    block = per * rows
+    heads = bias_w_ref.shape[0]
+    me = lax.axis_index("row")
+    group = lax.axis_index("groups")
+
+    def peer(t):
+        return lax.rem(me + (t % 2) * (n // 2) + t // 2, n)
+
+    def copy_to(src, dst, ssem, rsem, device):
+        return pltpu.make_async_remote_copy(
+            src_ref=src, dst_ref=dst, send_sem=ssem, recv_sem=rsem,
+            device_id=(group, device), device_id_type=MESH,
+        )
+
+    def exchange_start(send, got, ssem, rsem):
+        def body(t, _):
+            d = peer(t)
+            copy_to(send.at[d], got.at[me], ssem.at[d], rsem.at[me], d).start()
+            return 0
+        lax.fori_loop(1, n, body, 0)
+
+    def exchange_recv(send, got, ssem, rsem):
+        def body(t, _):
+            s = lax.rem(me + t, n)
+            copy_to(send.at[s], got.at[s], ssem.at[s], rsem.at[s], s).wait_recv()
+            return 0
+        lax.fori_loop(1, n, body, 0)
+
+    def exchange_sent(send, got, ssem, rsem):
+        def body(t, _):
+            d = lax.rem(me + t, n)
+            copy_to(send.at[d], got.at[me], ssem.at[d], rsem.at[me], d).wait_send()
+            return 0
+        lax.fori_loop(1, n, body, 0)
+
+    barrier = pltpu.get_barrier_semaphore()
+
+    def greet(t, _):
+        pl.semaphore_signal(barrier, inc=1, device_id=(group, lax.rem(me + t, n)), device_id_type=MESH)
+        return 0
+    lax.fori_loop(1, n, greet, 0)
+
+    def narrow(dst):
+        def body(d, _):
+            for q in range(wide.shape[0]):
+                part = wide[q, pl.ds(pl.multiple_of(d * block, 16), block), :]
+                dst[d, :, q * 128 : (q + 1) * 128] = part.astype(jnp.bfloat16)
+            return 0
+        lax.fori_loop(0, n, body, 0)
+
+    def widen(src):
+        def body(d, _):
+            for q in range(wide.shape[0]):
+                part = src[d, :, q * 128 : (q + 1) * 128].astype(jnp.float32)
+                wide[q, pl.ds(pl.multiple_of(d * block, 16), block), :] = part
+            return 0
+        lax.fori_loop(0, n, body, 0)
+
+    def gated(r, first, normed):
+        proj = matmul(tri_in_ref[first : first + 2 * width, :], normed)
+        value = sigmoid(proj[width:]) * proj[:width] * pm_ref[r]
+        scatter_rows(wide, r, rows, value)
+
+    def left_row(r, _):
+        normed = norm_rows(pair_ref[r].T).astype(jnp.bfloat16)
+        xn[r] = normed
+        gated(r, 0, normed)
+        return 0
+    lax.fori_loop(0, rows, left_row, 0)
+    narrow(left_send)
+    pl.semaphore_wait(barrier, n - 1)
+    exchange_start(left_send, left_got, left_ssem, left_rsem)
+
+    def right_row(r, _):
+        gated(r, 2 * width, xn[r])
+        return 0
+    lax.fori_loop(0, rows, right_row, 0)
+    narrow(right_send)
+    exchange_start(right_send, right_got, right_ssem, right_rsem)
+
+    left_got[me] = left_send[me]
+    right_got[me] = right_send[me]
+    exchange_recv(left_send, left_got, left_ssem, left_rsem)
+    widen(left_got)
+    for c in range(per):
+        for r in range(rows):
+            left_mat[c, r * n : (r + 1) * n, :] = gather_rows(wide, c * rows + r, n, block).astype(jnp.bfloat16)
+    exchange_recv(right_send, right_got, right_ssem, right_rsem)
+    widen(right_got)
+    for c in range(per):
+        for r in range(rows):
+            scatter_rows(square.at[c], r, rows, gather_rows(wide, c * rows + r, n, block))
+    for c in range(per):
+        tri = lax.dot_general(
+            left_mat[c], all_rows(square.at[c]).astype(jnp.bfloat16), (((1,), (1,)), ((), ())),
+            preferred_element_type=jnp.float32,
+        )
+        for r in range(rows):
+            scatter_rows(wide, c * rows + r, block, tri[r * n : (r + 1) * n])
+    narrow(tri_send)
+    exchange_start(tri_send, tri_got, tri_ssem, tri_rsem)
+    tri_got[me] = tri_send[me]
+    exchange_recv(tri_send, tri_got, tri_ssem, tri_rsem)
+    widen(tri_got)
+
+    def pair_row(r, _):
+        tnorm = norm_rows(gather_rows(wide, r, width, rows)).astype(jnp.bfloat16)
+        update = matmul(tri_out_ref[...], tnorm)
+        gating = sigmoid(matmul(gate_ref[...], xn[r]))
+        pair1 = pair_ref[r].T + pm_ref[r] * (gating * update)
+        pair1_ref[r] = pair1
+        yn = norm_rows(pair1).astype(jnp.bfloat16)
+        yn_ref[r] = yn
+        scatter_rows(bias_wide, r, rows, matmul(bias_w_ref[...], yn))
+        return 0
+    lax.fori_loop(0, rows, pair_row, 0)
+    bias_all[me] = all_rows(bias_wide).astype(jnp.bfloat16)
+
+    planes = n // PLANE
+    low = lax.rem(me, PLANE)
+    core = lax.rem(me, 2)
+    base = me - low
+    other = base + low - core + (1 - core)
+
+    def put(b, ssem, device):
+        return copy_to(bias_all.at[b], bias_all.at[b], ssem, bias_rsem.at[b], device)
+
+    def along(step):
+        return lax.rem(me + step * PLANE, n)
+
+    def beside(step):
+        return base + lax.rem(low + 2 * step, PLANE)
+
+    for step in range(1, planes):
+        put(me, z_ssem.at[step], along(step)).start()
+    for z in range(planes):
+        b = along(z)
+        if z:
+            put(b, z_ssem.at[z], me).wait_recv()
+        for step in range(1, PLANE // 2):
+            put(b, plane_ssem.at[z, step], beside(step)).start()
+        put(b, core_ssem.at[z, 0], other).start()
+    for z in range(planes):
+        for step in range(1, PLANE // 2):
+            b = lax.rem(beside(step) + z * PLANE, n)
+            put(b, plane_ssem.at[z, step], me).wait_recv()
+            put(b, core_ssem.at[z, step], other).start()
+    for z in range(planes):
+        for step in range(PLANE // 2):
+            b = lax.rem(base + lax.rem(low - core + (1 - core) + 2 * step, PLANE) + z * PLANE, n)
+            put(b, core_ssem.at[z, step], me).wait_recv()
+    for step in range(1, planes):
+        put(me, z_ssem.at[step], along(step)).wait_send()
+    for z in range(planes):
+        for step in range(PLANE // 2):
+            b = lax.rem(beside(step) + z * PLANE, n)
+            put(b, core_ssem.at[z, step], other).wait_send()
+            if step:
+                put(b, plane_ssem.at[z, step], beside(step)).wait_send()
+    bias_ref[...] = bias_all[...]
+    exchange_sent(left_send, left_got, left_ssem, left_rsem)
+    exchange_sent(right_send, right_got, right_ssem, right_rsem)
+    exchange_sent(tri_send, tri_got, tri_ssem, tri_rsem)
+
+
+def attention_kernel(rows, heads, bias_ref, hide_ref, pair1_ref, yn_ref, live_ref, att_in_ref, att_out_ref, out_ref, wide, square, bias_t):
+    n, block, residues = bias_ref.shape
+    width = yn_ref.shape[1]
+    hd = att_out_ref.shape[1]
+    size = hd // heads
+
+    @pl.when(pl.program_id(0) == 0)
+    def _():
+        for d in range(n):
+            for q in range(wide.shape[0]):
+                part = bias_ref[d, :, q * 128 : (q + 1) * 128].astype(jnp.float32)
+                wide[q, d * block : (d + 1) * block, :] = part * LOG2E
+        for h in range(heads):
+            for r in range(rows):
+                scatter_rows(square, r, rows, gather_rows(wide, h * rows + r, n, block))
+            bias_t[h] = (all_rows(square) + hide_ref[...]).T
+
+    qkvg = matmul(att_in_ref[...], yn_ref[0])
+    query = (qkvg[:hd] * (LOG2E / math.sqrt(size))).astype(jnp.bfloat16)
+    keys = qkvg[hd : 2 * hd].astype(jnp.bfloat16)
+    values = qkvg[2 * hd : 3 * hd].astype(jnp.bfloat16)
+    gates = sigmoid(qkvg[3 * hd :])
+    ones = jnp.ones((16, residues), jnp.bfloat16)
+    parts = []
+    for h in range(heads):
+        at = slice(h * size, (h + 1) * size)
+        scores = lax.dot_general(keys[at], query[at], (((0,), (0,)), ((), ())), preferred_element_type=jnp.float32)
+        scores = scores + bias_t[h]
+        probs = jnp.exp2(scores - jnp.max(scores, axis=0, keepdims=True)).astype(jnp.bfloat16)
+        mixed = matmul(jnp.concatenate([values[at], ones], axis=0), probs)
+        parts.append((mixed[:size] * (1.0 / mixed[size : size + 1]) * gates[at]).astype(jnp.bfloat16))
+    att = jnp.concatenate(parts, axis=0)
+    out = matmul(att_out_ref[...], att)
+    out_ref[0] = (pair1_ref[0] + live_ref[0] * out).T
+
+
+def fused(n, pair, mask, tri_in, tri_gate, tri_out, att_in, att_bias, att_out):
+    rows, residues, width = pair.shape
+    heads = att_bias.shape[1]
+    hd = att_out.shape[0]
+    per = width // n
+    block = per * rows
+    valid = mask.astype(jnp.float32)
+    row_valid = lax.dynamic_slice_in_dim(valid, lax.axis_index("row") * rows, rows, 0)
+    live = jnp.broadcast_to(row_valid[:, None, None], (rows, 1, residues))
+    pm = live * valid[None, None, :]
+    hide = jnp.where(mask > 0, 0.0, -jnp.inf).astype(jnp.float32)[None, :]
+    bf, f32 = jnp.bfloat16, jnp.float32
+    vmem = pl.BlockSpec(memory_space=pltpu.VMEM)
+    dma = pltpu.SemaphoreType.DMA
+    blocks = pltpu.VMEM((n, block, residues), bf)
+    planes = n // PLANE
+    pair1, yn, bias = pl.pallas_call(
+        functools.partial(triangle_kernel, n),
+        out_shape=(
+            jax.ShapeDtypeStruct((rows, width, residues), f32),
+            jax.ShapeDtypeStruct((rows, width, residues), bf),
+            jax.ShapeDtypeStruct((n, heads * rows, residues), bf),
+        ),
+        in_specs=[vmem] * 6,
+        out_specs=(vmem, vmem, vmem),
+        scratch_shapes=[
+            pltpu.VMEM((residues // 128, n * block, 128), f32),
+            pltpu.VMEM((per, residues // 128, residues, 128), f32),
+            pltpu.VMEM((rows, width, residues), bf),
+            blocks, blocks, blocks, blocks,
+            pltpu.VMEM((per, residues, residues), bf),
+            blocks, blocks,
+            pltpu.VMEM((n, heads * rows, residues), bf),
+            pltpu.VMEM((residues // 128, heads * rows, 128), f32),
+        ] + [dma((n,))] * 6 + [
+            dma((planes,)), dma((planes, PLANE // 2)), dma((planes, PLANE // 2)), dma((n,)),
+        ],
+        compiler_params=pltpu.CompilerParams(
+            collective_id=0, has_side_effects=True, vmem_limit_bytes=48 * 2**20
+        ),
+    )(pair, pm, tri_in.T, tri_gate.T, tri_out.T, att_bias.T)
+
+    def whole(shape):
+        return pl.BlockSpec(shape, lambda i: (0,) * len(shape))
+
+    def row(*shape):
+        return pl.BlockSpec((1,) + shape, lambda i: (i, 0, 0))
+
+    return pl.pallas_call(
+        functools.partial(attention_kernel, rows, heads),
+        grid=(rows,),
+        out_shape=jax.ShapeDtypeStruct((rows, residues, width), f32),
+        in_specs=[
+            whole((n, heads * rows, residues)), whole((1, residues)), row(width, residues), row(width, residues),
+            row(1, residues), whole((4 * hd, width)), whole((width, hd)),
+        ],
+        out_specs=row(residues, width),
+        scratch_shapes=[
+            pltpu.VMEM((residues // 128, n * heads * rows, 128), f32),
+            pltpu.VMEM((residues // 128, residues, 128), f32),
+            pltpu.VMEM((heads, residues, residues), f32),
+        ],
+        compiler_params=pltpu.CompilerParams(vmem_limit_bytes=48 * 2**20),
+    )(bias, hide, pair1, yn, live, att_in.T, att_out.T)
 
 
 def layer_norm(value):
@@ -76,8 +389,19 @@
 
 
 def solution(mesh):
+    n = mesh.shape["row"]
+
+    def per_shard(pair, mask, tri_in, tri_gate, tri_out, att_in, att_bias, att_out):
+        rows, residues, width = pair.shape
+        fits = (
+            width % n == 0 and n % 16 == 0 and n % PLANE == 0 and residues % 128 == 0
+            and (width // n * rows) % 16 == 0 and (att_bias.shape[1] * rows) % 16 == 0
+        )
+        run = functools.partial(fused, n) if fits else per_device
+        return run(pair, mask, tri_in, tri_gate, tri_out, att_in, att_bias, att_out)
+
     return jax.shard_map(
-        per_device,
+        per_shard,
         mesh=mesh,
         in_specs=(P(("groups", "row"), None, None), P("groups"), P(), P(), P(), P(), P(), P()),
         out_specs=P(("groups", "row"), None, None),

time: 266 us -> 145 us (0.55)
  waiting for transfers between devices: 140 us -> 0 us
  Pallas kernels: 0 us -> 136 us
  matrix products: 55.2 us -> 0 us
  local copies, waits for them, and re-layouts: 28.4 us -> 5.5 us
  starting transfers between devices: 15.4 us -> 0 us
  between operations: 13.7 us -> 0.06 us
  other arithmetic: 12.3 us -> 1.44 us
    pallas_call x0 -> x2, Pallas kernels: none -> 136 us  [the longest x1 110 us: fused(): pl.pallas_call(functools.partial(triangle_kernel, n), out_shape=(jax.Shap...]
    all_to_all x3 -> x0, waiting for transfers between devices: 93 us -> none  [the longest x1 34.8 us: per_device(): lax.all_to_all(right_by_channel, 'row', split_axis=0, concat_axis=1, tile...]
    all_gather x1 -> x0, waiting for transfers between devices: 46.9 us -> none  [per_device(): bias = lax.all_gather(local_bias, 'row', axis=1, tiled=True)]
    dot_general x8 -> x0, matrix products: 35.1 us -> none  [the longest x1 13.6 us: per_device(): jnp.einsum('ihjk,ikhd->ijhd', probs, values, preferred_element_type=jnp.f...]
    sub x1 -> x0, matrix products: 20.1 us -> none  [per_device(): probs = jax.nn.softmax(scores, axis=-1).astype(jnp.bfloat16)]
    all_to_all x3 -> x0, starting transfers between devices: 15.2 us -> none  [the longest x1 7.4 us: per_device(): lax.all_to_all(left_by_channel, 'row', split_axis=0, concat_axis=1, tiled...]
    transpose x4 -> x0, local copies, waits for them, and re-layouts: 9.64 us -> none  [the longest x2 4.63 us: per_device(): tri = jnp.transpose(tri_rows, (1, 2, 0))]
    convert_element_type x2 -> x0, local copies, waits for them, and re-layouts: 4.96 us -> none  [the longest x1 3.03 us: per_device(): scores = scores + bias.astype(jnp.float32)[None]]
  transfers between devices with their start and end apart: 4 -> 0, of which waited for: 4 -> 0; matrix products, arithmetic and copies ran while one was open for 7% -> 0% of each run, Pallas kernels for 0% -> 0%
where the time goes in v1:
time: 145 us; the launch traced here: 143 us
  Pallas kernels  136 us (94%)
  local copies, waits for them, and re-layouts  5.5 us (4%)
    pallas_call x1, Pallas kernels, fused(): pl.pallas_call(functools.partial(triangle_kernel, n), out_shape=(jax.Shap...  110 us
    pallas_call x1, Pallas kernels, fused(): pl.pallas_call(functools.partial(attention_kernel, rows, heads), grid=(ro...  25.7 us
    unnamed x7, local copies, waits for them, and re-layouts  5.34 us

profile of v1, /device:TPU:0, one launch (start us, length us, event | category | flops | bytes accessed | tf_op | source)
XLA Modules:
  0.0 142.9 jit_solution(629181759242668684)
XLA Ops:
  0.0 0.7 convert_element_type.3
  0.7 0.1 dynamic_slice.3
  0.8 0.7 compare_select_fusion
  1.5 0.1 broadcast_multiply_fusion.pm_ref
  1.5 0.1 broadcast_in_dim.18.live_ref
  1.6 0.9 copy.10
  2.5 0.9 copy.11
  3.4 0.9 copy.13
  4.2 1.0 copy.9
  5.3 1.0 copy.12
  6.3 0.0 copy-start
  6.3 0.7 copy-done
  7.0 110.2 %shard_map.82 = (f32[12,128,384]{2,1,0:T(8,128)S(1)}, bf16[12,128,384]{2,1,0:T(8,128)(2,1)S(1)}, bf16[32,48,384]{2,1,0:T(8,128)(2,1)S(1)}) custom-call(f32[12,384,128]{2,1,0:T(8,128)} %pair_ref.1, f32[12,1,384]{2,1,0:T(1,128)S(1)} %broadcast_multiply_fusion.pm_ref, bf16[512,128]{1,0:T(8,128)(2,1)S(1)} %bitcast.7, bf16[128,128]{1,0:T(8,128)(2,1)S(1)} %bitcast.9, ...), custom_call_target="tpu_custom_call" | custom-call | tf_op jit(solution)/shard_map/pallas_call | solution.py:270
  117.2 25.7 %shard_map.83 = f32[12,384,128]{2,1,0:T(8,128)} custom-call(bf16[32,48,384]{2,1,0:T(8,128)(2,1)S(1)} %get-tuple-element.8.bias_ref, f32[1,384]{1,0:T(1,128)S(1)} %broadcast_in_dim.21.hide_ref, f32[12,128,384]{2,1,0:T(8,128)S(1)} %get-tuple-element.9.pair1_ref, bf16[12,128,384]{2,1,0:T(8,128)(2,1)S(1)} %get-tuple-element.10.yn_ref, ...), custom_call_target="tpu_custom_call" | custom-call | tf_op jit(solution)/shard_map/pallas_call | solution.py:302
  (1 shorter events, 0.0 us)
Async XLA Ops:
  6.3 0.7 copy-start

commit v2 on v0

--- a/solution.py
+++ b/solution.py
@@ -1,7 +1,386 @@
+import functools
+import math
+
 import jax
 import jax.numpy as jnp
 from jax import lax
+from jax.experimental import pallas as pl
+from jax.experimental.pallas import tpu as pltpu
 from jax.sharding import PartitionSpec as P
+
+EPS = 1e-05
+LOG2E = math.log2(math.e)
+MESH = pl.DeviceIdType.MESH
+PLANE = 8
+
+
+def sigmoid(value):
+    return 0.5 * jnp.tanh(0.5 * value) + 0.5
+
+
+def norm_rows(value):
+    center = value - jnp.mean(value, axis=0, keepdims=True)
+    return center * lax.rsqrt(jnp.mean(center * center, axis=0, keepdims=True) + EPS)
+
+
+def scatter_rows(ref, first, stride, value):
+    for q in range(ref.shape[0]):
+        ref[q, pl.ds(first, value.shape[0], stride=stride), :] = value[:, q * 128 : (q + 1) * 128]
+
+
+def gather_rows(ref, first, count, stride):
+    parts = [ref[q, pl.ds(first, count, stride=stride), :] for q in range(ref.shape[0])]
+    return jnp.concatenate(parts, axis=1)
+
+
+def all_rows(ref):
+    return jnp.concatenate([ref[q] for q in range(ref.shape[0])], axis=1)
+
+
+def matmul(a, b):
+    return jnp.dot(a, b, preferred_element_type=jnp.float32)
+
+
+def to_t(ref):
+    return ref[...].astype(jnp.float32).T.astype(jnp.bfloat16)
+
+
+def triangle_kernel(
+    n, chunk, heads,
+    pair_ref, mask_ref, live_ref, tri_in_ref, gate_ref, tri_out_ref, att_in_ref, bias_w_ref,
+    pair1_ref, qkv_ref, g_ref, bias_ref,
+    wide, bias_wide, square, right_mat, xn, yn, gating, tri_in_t, gate_t, tri_out_t, att_in_t,
+    left_send, right_send, tri_send, left_got, right_got, tri_got, bias_all,
+    left_ssem, left_rsem, right_ssem, right_rsem, tri_ssem, tri_rsem,
+    z_ssem, plane_ssem, core_ssem, bias_rsem,
+):
+    rows, residues, width = pair_ref.shape
+    per = width // n
+    block = per * chunk
+    chunks = rows // chunk
+    hd = g_ref.shape[1]
+    tiles = residues // 128
+    me = lax.axis_index("row")
+    group = lax.axis_index("groups")
+
+    def loop(low, high, body):
+        def step(i, _):
+            body(i)
+            return 0
+        lax.fori_loop(low, high, step, 0)
+
+    def peer(t):
+        return lax.rem(me + (t % 2) * (n // 2) + t // 2, n)
+
+    def copy_to(src, dst, ssem, rsem, device):
+        return pltpu.make_async_remote_copy(
+            src_ref=src, dst_ref=dst, send_sem=ssem, recv_sem=rsem,
+            device_id=(group, device), device_id_type=MESH,
+        )
+
+    def outgoing(plan, u, d):
+        send, got, ssem, rsem = plan
+        return copy_to(send.at[u, d], got.at[u, me], ssem.at[u, d], rsem.at[u, me], d)
+
+    def incoming(plan, u, s):
+        send, got, ssem, rsem = plan
+        return copy_to(send.at[u, s], got.at[u, s], ssem.at[u, s], rsem.at[u, s], s)
+
+    left = (left_send, left_got, left_ssem, left_rsem)
+    right = (right_send, right_got, right_ssem, right_rsem)
+    back = (tri_send, tri_got, tri_ssem, tri_rsem)
+
+    def send_chunk(plan, u):
+        def narrow(d):
+            for q in range(tiles):
+                part = wide[q, pl.ds(pl.multiple_of(d * block, 16), block), :]
+                plan[0][u, d, :, q * 128 : (q + 1) * 128] = part.astype(jnp.bfloat16)
+        loop(0, n, narrow)
+        loop(1, n, lambda t: outgoing(plan, u, peer(t)).start())
+        plan[1][u, me] = plan[0][u, me]
+
+    def receive_chunk(plan, u):
+        loop(1, n, lambda t: incoming(plan, u, lax.rem(me + t, n)).wait_recv())
+
+        def widen(s):
+            for q in range(tiles):
+                part = plan[1][u, s, :, q * 128 : (q + 1) * 128].astype(jnp.float32)
+                wide[q, pl.ds(pl.multiple_of(s * block, 16), block), :] = part
+        loop(0, n, widen)
+
+    barrier = pltpu.get_barrier_semaphore()
+    loop(1, n, lambda t: pl.semaphore_signal(
+        barrier, inc=1, device_id=(group, lax.rem(me + t, n)), device_id_type=MESH))
+
+    valid = mask_ref[...].astype(jnp.float32)
+
+    def pm(r):
+        return valid * live_ref[0, me * rows + r].astype(jnp.float32)
+
+    tri_in_t[...] = to_t(tri_in_ref)
+
+    def gated(r, place, first):
+        proj = matmul(tri_in_t[first : first + 2 * width, :], xn[r])
+        value = sigmoid(proj[width:]) * proj[:width] * pm(r)
+        scatter_rows(wide, place, chunk, value)
+
+    for u in range(chunks):
+        def right_row(t):
+            r = u * chunk + t
+            pair_t = pair_ref[r].T
+            pair1_ref[r] = pair_t
+            xn[r] = norm_rows(pair_t).astype(jnp.bfloat16)
+            gated(r, t, 2 * width)
+        loop(0, chunk, right_row)
+        if u == 0:
+            pl.semaphore_wait(barrier, n - 1)
+        send_chunk(right, u)
+    for u in range(chunks):
+        loop(0, chunk, lambda t: gated(u * chunk + t, t, 0))
+        send_chunk(left, u)
+
+    gate_t[...] = to_t(gate_ref)
+    tri_out_t[...] = to_t(tri_out_ref)
+    att_in_t[...] = to_t(att_in_ref)
+
+    def gate_row(r):
+        gating[r] = sigmoid(matmul(gate_t[...], xn[r])) * pm(r)
+    loop(0, rows, gate_row)
+
+    for u in range(chunks):
+        receive_chunk(right, u)
+        for c in range(per):
+            for t in range(chunk):
+                part = gather_rows(wide, c * chunk + t, n, block)
+                scatter_rows(square.at[c], u * chunk + t, rows, part)
+    for c in range(per):
+        right_mat[c] = all_rows(square.at[c]).astype(jnp.bfloat16)
+    for u in range(chunks):
+        receive_chunk(left, u)
+        for c in range(per):
+            lefts = [gather_rows(wide, c * chunk + t, n, block) for t in range(chunk)]
+            tri = lax.dot_general(
+                jnp.concatenate(lefts, axis=0).astype(jnp.bfloat16), right_mat[c],
+                (((1,), (1,)), ((), ())), preferred_element_type=jnp.float32,
+            )
+            for t in range(chunk):
+                scatter_rows(wide, c * chunk + t, block, tri[t * n : (t + 1) * n])
+        send_chunk(back, u)
+
+    planes = n // PLANE
+    low = lax.rem(me, PLANE)
+    base = me - low
+    twin_low = low - lax.rem(me, 2) + (1 - lax.rem(me, 2))
+    twin = base + twin_low
+
+    def put(u, b, ssem, device):
+        return copy_to(bias_all.at[u, b], bias_all.at[u, b], ssem, bias_rsem.at[u, b], device)
+
+    def along(step):
+        return lax.rem(me + step * PLANE, n)
+
+    def beside(step):
+        return base + lax.rem(low + 2 * step, PLANE)
+
+    def bias_first(u):
+        for step in range(1, planes):
+            put(u, me, z_ssem.at[u, step], along(step)).start()
+
+    def bias_second(u):
+        for z in range(planes):
+            b = along(z)
+            if z:
+                put(u, b, z_ssem.at[u, z], me).wait_recv()
+            for step in range(1, PLANE // 2):
+                put(u, b, plane_ssem.at[u, z, step], beside(step)).start()
+            put(u, b, core_ssem.at[u, z, 0], twin).start()
+
+    def bias_third(u):
+        for z in range(planes):
+            for step in range(1, PLANE // 2):
+                b = lax.rem(beside(step) + z * PLANE, n)
+                put(u, b, plane_ssem.at[u, z, step], me).wait_recv()
+                put(u, b, core_ssem.at[u, z, step], twin).start()
+
+    def bias_last(u):
+        for z in range(planes):
+            for step in range(PLANE // 2):
+                b = lax.rem(base + lax.rem(twin_low + 2 * step, PLANE) + z * PLANE, n)
+                put(u, b, core_ssem.at[u, z, step], me).wait_recv()
+
+    def bias_sent(u):
+        for step in range(1, planes):
+            put(u, me, z_ssem.at[u, step], along(step)).wait_send()
+        for z in range(planes):
+            for step in range(PLANE // 2):
+                b = lax.rem(beside(step) + z * PLANE, n)
+                put(u, b, core_ssem.at[u, z, step], twin).wait_send()
+                if step:
+                    put(u, along(z), plane_ssem.at[u, z, step], beside(step)).wait_send()
+
+    scale = LOG2E / math.sqrt(hd // heads)
+
+    def qkvg_row(r):
+        qkvg = matmul(att_in_t[...], yn[r])
+        qkv_ref[r, :hd, :] = (qkvg[:hd] * scale).astype(jnp.bfloat16)
+        qkv_ref[r, hd:, :] = qkvg[hd : 3 * hd].astype(jnp.bfloat16)
+        g_ref[r] = sigmoid(qkvg[3 * hd :])
+
+    for u in range(chunks):
+        receive_chunk(back, u)
+
+        def pair_row(t):
+            r = u * chunk + t
+            tnorm = norm_rows(gather_rows(wide, t, width, chunk)).astype(jnp.bfloat16)
+            pair1 = pair1_ref[r] + gating[r] * matmul(tri_out_t[...], tnorm)
+            pair1_ref[r] = pair1
+            fresh = norm_rows(pair1).astype(jnp.bfloat16)
+            yn[r] = fresh
+            scatter_rows(bias_wide, t, chunk, matmul(bias_w_ref[...], fresh))
+        loop(0, chunk, pair_row)
+        bias_all[u, me] = all_rows(bias_wide).astype(jnp.bfloat16)
+        bias_first(u)
+        if u < chunks - 1:
+            loop(u * chunk, (u + 1) * chunk, qkvg_row)
+        if u >= 1:
+            bias_second(u - 1)
+        if u >= 2:
+            bias_third(u - 2)
+    done = (chunks - 1) * chunk
+    half = chunk // 2
+    loop(done, done + half, qkvg_row)
+    bias_second(chunks - 1)
+    if chunks >= 2:
+        bias_third(chunks - 2)
+    loop(done + half, done + chunk, qkvg_row)
+    bias_third(chunks - 1)
+    for u in range(chunks):
+        bias_last(u)
+        bias_ref[u] = bias_all[u]
+    for u in range(chunks):
+        bias_sent(u)
+        for plan in (right, left, back):
+            loop(1, n, lambda t: outgoing(plan, u, lax.rem(me + t, n)).wait_send())
+
+
+def attention_kernel(rows, heads, bias_ref, mask_ref, live_ref, pair1_ref, qkv_ref, g_ref, att_out_ref, out_ref, wide, square, bias_t, out_t):
+    chunks, n, block, residues = bias_ref.shape
+    hd = g_ref.shape[1]
+    size = hd // heads
+    chunk = block // heads
+
+    @pl.when(pl.program_id(0) == 0)
+    def _():
+        out_t[...] = to_t(att_out_ref)
+        for u in range(chunks):
+            for d in range(n):
+                for q in range(wide.shape[0]):
+                    part = bias_ref[u, d, :, q * 128 : (q + 1) * 128].astype(jnp.float32)
+                    wide[q, d * block : (d + 1) * block, :] = part * LOG2E
+            for h in range(heads):
+                for t in range(chunk):
+                    scatter_rows(square.at[h], u * chunk + t, rows, gather_rows(wide, h * chunk + t, n, block))
+        hide = jnp.where(mask_ref[...] > 0, 0.0, -jnp.inf)
+        for h in range(heads):
+            bias_t[h] = (all_rows(square.at[h]) + hide).T
+
+    ones = jnp.ones((16, residues), jnp.bfloat16)
+    parts = []
+    for h in range(heads):
+        first = h * size
+        query = qkv_ref[0, first : first + size, :]
+        keys = qkv_ref[0, hd + first : hd + first + size, :]
+        values = qkv_ref[0, 2 * hd + first : 2 * hd + first + size, :]
+        scores = lax.dot_general(keys, query, (((0,), (0,)), ((), ())), preferred_element_type=jnp.float32)
+        scores = scores + bias_t[h]
+        probs = jnp.exp2(scores - jnp.max(scores, axis=0, keepdims=True)).astype(jnp.bfloat16)
+        mixed = matmul(jnp.concatenate([values, ones], axis=0), probs)
+        gates = g_ref[0, first : first + size, :]
+        parts.append((mixed[:size] * (1.0 / mixed[size : size + 1]) * gates).astype(jnp.bfloat16))
+    out = matmul(out_t[...], jnp.concatenate(parts, axis=0))
+    live = live_ref[0, lax.axis_index("row") * rows + pl.program_id(0)].astype(jnp.float32)
+    out_ref[0] = (pair1_ref[0] + live * out).T
+
+
+def chunk_rows(n, rows, width, heads):
+    per = width // n
+    for chunk in range(1, rows + 1):
+        if rows % chunk == 0 and (per * chunk) % 16 == 0 and (heads * chunk) % 16 == 0:
+            return chunk
+    return 0
+
+
+def fused(n, pair, mask, tri_in, tri_gate, tri_out, att_in, att_bias, att_out):
+    rows, residues, width = pair.shape
+    heads = att_bias.shape[1]
+    hd = att_out.shape[0]
+    per = width // n
+    chunk = chunk_rows(n, rows, width, heads)
+    chunks = rows // chunk
+    tiles = residues // 128
+    planes = n // PLANE
+    flat = mask.reshape(1, residues)
+    bf, f32 = jnp.bfloat16, jnp.float32
+    vmem = pl.BlockSpec(memory_space=pltpu.VMEM)
+    smem = pl.BlockSpec(memory_space=pltpu.SMEM)
+    dma = pltpu.SemaphoreType.DMA
+    blocks = pltpu.VMEM((chunks, n, per * chunk, residues), bf)
+    side = PLANE // 2
+    pair1, qkv, gates, bias = pl.pallas_call(
+        functools.partial(triangle_kernel, n, chunk, heads),
+        out_shape=(
+            jax.ShapeDtypeStruct((rows, width, residues), f32),
+            jax.ShapeDtypeStruct((rows, 3 * hd, residues), bf),
+            jax.ShapeDtypeStruct((rows, hd, residues), f32),
+            jax.ShapeDtypeStruct((chunks, n, heads * chunk, residues), bf),
+        ),
+        in_specs=[vmem, vmem, smem] + [vmem] * 5,
+        out_specs=(vmem,) * 4,
+        scratch_shapes=[
+            pltpu.VMEM((tiles, width * chunk, 128), f32),
+            pltpu.VMEM((tiles, heads * chunk, 128), f32),
+            pltpu.VMEM((per, tiles, residues, 128), f32),
+            pltpu.VMEM((per, residues, residues), bf),
+            pltpu.VMEM((rows, width, residues), bf),
+            pltpu.VMEM((rows, width, residues), bf),
+            pltpu.VMEM((rows, width, residues), f32),
+            pltpu.VMEM((4 * width, width), bf),
+            pltpu.VMEM((width, width), bf),
+            pltpu.VMEM((width, width), bf),
+            pltpu.VMEM((4 * hd, width), bf),
+        ] + [blocks] * 6 + [
+            pltpu.VMEM((chunks, n, heads * chunk, residues), bf),
+        ] + [dma((chunks, n))] * 6 + [
+            dma((chunks, planes)), dma((chunks, planes, side)), dma((chunks, planes, side)), dma((chunks, n)),
+        ],
+        compiler_params=pltpu.CompilerParams(
+            collective_id=0, has_side_effects=True, vmem_limit_bytes=56 * 2**20
+        ),
+    )(pair, flat, flat, tri_in, tri_gate, tri_out, att_in, att_bias.T)
+
+    def whole(shape):
+        return pl.BlockSpec(shape, lambda i: (0,) * len(shape))
+
+    def row(*shape):
+        return pl.BlockSpec((1,) + shape, lambda i: (i, 0, 0))
+
+    return pl.pallas_call(
+        functools.partial(attention_kernel, rows, heads),
+        grid=(rows,),
+        out_shape=jax.ShapeDtypeStruct((rows, residues, width), f32),
+        in_specs=[
+            whole((chunks, n, heads * chunk, residues)), whole((1, residues)), smem,
+            row(width, residues), row(3 * hd, residues), row(hd, residues), whole((hd, width)),
+        ],
+        out_specs=row(residues, width),
+        scratch_shapes=[
+            pltpu.VMEM((tiles, n * heads * chunk, 128), f32),
+            pltpu.VMEM((heads, tiles, residues, 128), f32),
+            pltpu.VMEM((heads, residues, residues), f32),
+            pltpu.VMEM((width, hd), bf),
+        ],
+        compiler_params=pltpu.CompilerParams(vmem_limit_bytes=48 * 2**20),
+    )(bias, flat, flat, pair1, qkv, gates, att_out)
 
 
 def layer_norm(value):
@@ -76,8 +455,19 @@
 
 
 def solution(mesh):
+    n = mesh.shape["row"]
+
+    def per_shard(pair, mask, tri_in, tri_gate, tri_out, att_in, att_bias, att_out):
+        rows, residues, width = pair.shape
+        fits = (
+            width % n == 0 and n % PLANE == 0 and n % 16 == 0 and residues % 128 == 0
+            and chunk_rows(n, rows, width, att_bias.shape[1]) > 0
+        )
+        run = functools.partial(fused, n) if fits else per_device
+        return run(pair, mask, tri_in, tri_gate, tri_out, att_in, att_bias, att_out)
+
     return jax.shard_map(
-        per_device,
+        per_shard,
         mesh=mesh,
         in_specs=(P(("groups", "row"), None, None), P("groups"), P(), P(), P(), P(), P(), P()),
         out_specs=P(("groups", "row"), None, None),

time: 266 us -> 143 us (0.54)
  waiting for transfers between devices: 140 us -> 0 us
  Pallas kernels: 0 us -> 136 us
  matrix products: 55.2 us -> 0 us
  local copies, waits for them, and re-layouts: 28.4 us -> 5.85 us
  starting transfers between devices: 15.4 us -> 0 us
  between operations: 13.7 us -> 0.04 us
  other arithmetic: 12.3 us -> 0 us
    pallas_call x0 -> x2, Pallas kernels: none -> 136 us  [the longest x1 112 us: fused(): pl.pallas_call(functools.partial(triangle_kernel, n, chunk, heads), out_s...]
    all_to_all x3 -> x0, waiting for transfers between devices: 93 us -> none  [the longest x1 34.8 us: per_device(): lax.all_to_all(right_by_channel, 'row', split_axis=0, concat_axis=1, tile...]
    all_gather x1 -> x0, waiting for transfers between devices: 46.9 us -> none  [per_device(): bias = lax.all_gather(local_bias, 'row', axis=1, tiled=True)]
    dot_general x8 -> x0, matrix products: 35.1 us -> none  [the longest x1 13.6 us: per_device(): jnp.einsum('ihjk,ikhd->ijhd', probs, values, preferred_element_type=jnp.f...]
    sub x1 -> x0, matrix products: 20.1 us -> none  [per_device(): probs = jax.nn.softmax(scores, axis=-1).astype(jnp.bfloat16)]
    all_to_all x3 -> x0, starting transfers between devices: 15.2 us -> none  [the longest x1 7.4 us: per_device(): lax.all_to_all(left_by_channel, 'row', split_axis=0, concat_axis=1, tiled...]
    transpose x4 -> x0, local copies, waits for them, and re-layouts: 9.64 us -> none  [the longest x2 4.63 us: per_device(): tri = jnp.transpose(tri_rows, (1, 2, 0))]
    convert_element_type x2 -> x0, local copies, waits for them, and re-layouts: 4.96 us -> none  [the longest x1 3.03 us: per_device(): scores = scores + bias.astype(jnp.float32)[None]]
  transfers between devices with their start and end apart: 4 -> 0, of which waited for: 4 -> 0; matrix products, arithmetic and copies ran while one was open for 7% -> 0% of each run, Pallas kernels for 0% -> 0%
where the time goes in v2:
time: 143 us; the launch traced here: 142 us
  Pallas kernels  136 us (95%)
  local copies, waits for them, and re-layouts  5.85 us (4%)
    pallas_call x1, Pallas kernels, fused(): pl.pallas_call(functools.partial(triangle_kernel, n, chunk, heads), out_s...  112 us
    pallas_call x1, Pallas kernels, fused(): pl.pallas_call(functools.partial(attention_kernel, rows, heads), grid=(ro...  24.7 us
    unnamed x10, local copies, waits for them, and re-layouts  4.6 us

profile of v2, /device:TPU:0, one launch (start us, length us, event | category | flops | bytes accessed | tf_op | source)
XLA Modules:
  0.0 142.1 jit_solution(163407978572287200)
XLA Ops:
  0.0 0.0 copy-start.4
  0.0 1.3 reshape.3.mask_ref.live_ref
  1.3 0.0 copy-start.3
  1.3 111.5 %shard_map.82 = (f32[12,128,384]{2,1,0:T(8,128)}, bf16[12,384,384]{2,1,0:T(8,128)(2,1)}, f32[12,128,384]{2,1,0:T(8,128)}, bf16[3,32,16,384]{3,2,1,0:T(8,128)(2,1)}) custom-call(f32[12,384,128]{2,1,0:T(8,128)} %pair_ref.1, s32[1,384]{1,0:T(1,128)} %reshape.3.mask_ref.live_ref, s32[1,384]{1,0:T(1,128)} %reshape.3.mask_ref.live_ref, ...), custom_call_target="tpu_custom_call" | custom-call | tf_op jit(solution)/shard_map/pallas_call | solution.py:329
  112.8 0.0 copy-done.4
  112.8 0.0 copy-done.3
  112.8 0.0 copy-start
  112.8 1.7 %copy-done = f32[12,128,384]{2,1,0:T(8,128)S(1)} copy-done((f32[12,128,384]{2,1,0:T(8,128)S(1)}, f32[12,128,384]{2,1,0:T(8,128)}, u32[]{:S(2)}) %copy-start) | copy-done | bytes 2359320
  114.5 0.0 copy-start.1
  114.5 1.7 %copy-done.1 = f32[12,128,384]{2,1,0:T(8,128)S(1)} copy-done((f32[12,128,384]{2,1,0:T(8,128)S(1)}, f32[12,128,384]{2,1,0:T(8,128)}, u32[]{:S(2)}) %copy-start.1) | copy-done | bytes 2359320
  116.1 0.0 copy-start.2
  116.1 1.3 copy-done.2
  117.4 24.7 %shard_map.83 = f32[12,384,128]{2,1,0:T(8,128)} custom-call(bf16[3,32,16,384]{3,2,1,0:T(8,128)(2,1)S(1)} %copy-done.2, s32[1,384]{1,0:T(1,128)S(1)} %copy-done.3, s32[1,384]{1,0:T(1,128)S(1)} %copy-done.3, f32[12,128,384]{2,1,0:T(8,128)S(1)} %copy-done, bf16[12,384,384]{2,1,0:T(8,128)(2,1)} %get-tuple-element.11.qkv_ref, f32[12,128,384]{2,1,0:T(8,128)S(1)} %copy-done.1, ...), custom_call_target="tpu_custom_call" | custom-call | tf_op jit(solution)/shard_map/pallas_call | solution.py:367
Async XLA Ops:
  0.0 112.8 %copy-start.4 = (bf16[128,128]{1,0:T(8,128)(2,1)S(1)}, bf16[128,128]{1,0:T(8,128)(2,1)}, u32[]{:S(2)}) copy-start(bf16[128,128]{1,0:T(8,128)(2,1)} %att_out_ref.1) | copy-start | bytes 98308
  1.3 111.5 %copy-start.3 = (s32[1,384]{1,0:T(1,128)S(1)}, s32[1,384]{1,0:T(1,128)}, u32[]{:S(2)}) copy-start(s32[1,384]{1,0:T(1,128)} %reshape.3.mask_ref.live_ref) | copy-start | bytes 4612
  112.8 1.7 %copy-start = (f32[12,128,384]{2,1,0:T(8,128)S(1)}, f32[12,128,384]{2,1,0:T(8,128)}, u32[]{:S(2)}) copy-start(f32[12,128,384]{2,1,0:T(8,128)} %get-tuple-element.10.pair1_ref) | copy-start | bytes 7077892
  114.5 1.7 %copy-start.1 = (f32[12,128,384]{2,1,0:T(8,128)S(1)}, f32[12,128,384]{2,1,0:T(8,128)}, u32[]{:S(2)}) copy-start(f32[12,128,384]{2,1,0:T(8,128)} %get-tuple-element.12.g_ref) | copy-start | bytes 7077892
  116.1 1.3 copy-start.2

commit v3 on v2

--- a/solution.py
+++ b/solution.py
@@ -49,7 +49,7 @@
     n, chunk, heads,
     pair_ref, mask_ref, live_ref, tri_in_ref, gate_ref, tri_out_ref, att_in_ref, bias_w_ref,
     pair1_ref, qkv_ref, g_ref, bias_ref,
-    wide, bias_wide, square, right_mat, xn, yn, gating, tri_in_t, gate_t, tri_out_t, att_in_t,
+    wide, bias_wide, bias_rows, right_mat, xn, yn, gating, tri_in_t, gate_t, tri_out_t, att_in_t,
     left_send, right_send, tri_send, left_got, right_got, tri_got, bias_all,
     left_ssem, left_rsem, right_ssem, right_rsem, tri_ssem, tri_rsem,
     z_ssem, plane_ssem, core_ssem, bias_rsem,
@@ -127,7 +127,9 @@
     for u in range(chunks):
         def right_row(t):
             r = u * chunk + t
-            pair_t = pair_ref[r].T
+            pair_t = jnp.concatenate(
+                [pair_ref[r, pl.ds(rr, n, stride=rows), :] for rr in range(rows)], axis=0
+            ).T
             pair1_ref[r] = pair_t
             xn[r] = norm_rows(pair_t).astype(jnp.bfloat16)
             gated(r, t, 2 * width)
@@ -151,10 +153,9 @@
         receive_chunk(right, u)
         for c in range(per):
             for t in range(chunk):
+                first = (u * chunk + t) * n
                 part = gather_rows(wide, c * chunk + t, n, block)
-                scatter_rows(square.at[c], u * chunk + t, rows, part)
-    for c in range(per):
-        right_mat[c] = all_rows(square.at[c]).astype(jnp.bfloat16)
+                right_mat[c, first : first + n, :] = part.astype(jnp.bfloat16)
     for u in range(chunks):
         receive_chunk(left, u)
         for c in range(per):
@@ -207,6 +208,21 @@
             for step in range(PLANE // 2):
                 b = lax.rem(base + lax.rem(twin_low + 2 * step, PLANE) + z * PLANE, n)
                 put(u, b, core_ssem.at[u, z, step], me).wait_recv()
+
+    hide = jnp.where(mask_ref[...] > 0, 0.0, -jnp.inf)
+
+    def bias_finish(u):
+        bias_last(u)
+        tall = heads * chunk
+
+        def widen(s):
+            for q in range(tiles):
+                part = bias_all[u, s, :, q * 128 : (q + 1) * 128].astype(jnp.float32)
+                bias_rows[q, pl.ds(pl.multiple_of(s * tall, 16), tall), :] = part * LOG2E
+        loop(0, n, widen)
+        for h in range(heads):
+            part = jnp.concatenate([gather_rows(bias_rows, h * chunk + t, n, tall) for t in range(chunk)], axis=0)
+            bias_ref[h, :, u * chunk * n : (u + 1) * chunk * n] = (part + hide).T
 
     def bias_sent(u):
         for step in range(1, planes):
@@ -248,41 +264,31 @@
             bias_third(u - 2)
     done = (chunks - 1) * chunk
     half = chunk // 2
+    for u in range(chunks - 2):
+        bias_finish(u)
+    bias_second(chunks - 1)
     loop(done, done + half, qkvg_row)
-    bias_second(chunks - 1)
     if chunks >= 2:
         bias_third(chunks - 2)
+    bias_third(chunks - 1)
     loop(done + half, done + chunk, qkvg_row)
-    bias_third(chunks - 1)
-    for u in range(chunks):
-        bias_last(u)
-        bias_ref[u] = bias_all[u]
+    for u in range(max(chunks - 2, 0), chunks):
+        bias_finish(u)
     for u in range(chunks):
         bias_sent(u)
         for plan in (right, left, back):
             loop(1, n, lambda t: outgoing(plan, u, lax.rem(me + t, n)).wait_send())
 
 
-def attention_kernel(rows, heads, bias_ref, mask_ref, live_ref, pair1_ref, qkv_ref, g_ref, att_out_ref, out_ref, wide, square, bias_t, out_t):
-    chunks, n, block, residues = bias_ref.shape
+def attention_kernel(n, bias_ref, live_ref, pair1_ref, qkv_ref, g_ref, att_out_ref, out_ref, out_t):
+    heads, residues, _ = bias_ref.shape
+    rows = residues // n
     hd = g_ref.shape[1]
     size = hd // heads
-    chunk = block // heads
 
     @pl.when(pl.program_id(0) == 0)
     def _():
         out_t[...] = to_t(att_out_ref)
-        for u in range(chunks):
-            for d in range(n):
-                for q in range(wide.shape[0]):
-                    part = bias_ref[u, d, :, q * 128 : (q + 1) * 128].astype(jnp.float32)
-                    wide[q, d * block : (d + 1) * block, :] = part * LOG2E
-            for h in range(heads):
-                for t in range(chunk):
-                    scatter_rows(square.at[h], u * chunk + t, rows, gather_rows(wide, h * chunk + t, n, block))
-        hide = jnp.where(mask_ref[...] > 0, 0.0, -jnp.inf)
-        for h in range(heads):
-            bias_t[h] = (all_rows(square.at[h]) + hide).T
 
     ones = jnp.ones((16, residues), jnp.bfloat16)
     parts = []
@@ -292,20 +298,22 @@
         keys = qkv_ref[0, hd + first : hd + first + size, :]
         values = qkv_ref[0, 2 * hd + first : 2 * hd + first + size, :]
         scores = lax.dot_general(keys, query, (((0,), (0,)), ((), ())), preferred_element_type=jnp.float32)
-        scores = scores + bias_t[h]
+        scores = scores + bias_ref[h]
         probs = jnp.exp2(scores - jnp.max(scores, axis=0, keepdims=True)).astype(jnp.bfloat16)
         mixed = matmul(jnp.concatenate([values, ones], axis=0), probs)
         gates = g_ref[0, first : first + size, :]
         parts.append((mixed[:size] * (1.0 / mixed[size : size + 1]) * gates).astype(jnp.bfloat16))
     out = matmul(out_t[...], jnp.concatenate(parts, axis=0))
     live = live_ref[0, lax.axis_index("row") * rows + pl.program_id(0)].astype(jnp.float32)
-    out_ref[0] = (pair1_ref[0] + live * out).T
+    new = (pair1_ref[0] + live * out).T
+    for r in range(rows):
+        out_ref[0, pl.ds(r, n, stride=rows), :] = new[r * n : (r + 1) * n]
 
 
 def chunk_rows(n, rows, width, heads):
     per = width // n
     for chunk in range(1, rows + 1):
-        if rows % chunk == 0 and (per * chunk) % 16 == 0 and (heads * chunk) % 16 == 0:
+        if rows % chunk == 0 and (chunk * n) % 128 == 0 and (per * chunk) % 16 == 0 and (heads * chunk) % 16 == 0:
             return chunk
     return 0
 
@@ -320,6 +328,7 @@
     tiles = residues // 128
     planes = n // PLANE
     flat = mask.reshape(1, residues)
+    turned = mask.reshape(n, rows).T.reshape(1, residues)
     bf, f32 = jnp.bfloat16, jnp.float32
     vmem = pl.BlockSpec(memory_space=pltpu.VMEM)
     smem = pl.BlockSpec(memory_space=pltpu.SMEM)
@@ -332,14 +341,14 @@
             jax.ShapeDtypeStruct((rows, width, residues), f32),
             jax.ShapeDtypeStruct((rows, 3 * hd, residues), bf),
             jax.ShapeDtypeStruct((rows, hd, residues), f32),
-            jax.ShapeDtypeStruct((chunks, n, heads * chunk, residues), bf),
+            jax.ShapeDtypeStruct((heads, residues, residues), f32),
         ),
         in_specs=[vmem, vmem, smem] + [vmem] * 5,
         out_specs=(vmem,) * 4,
         scratch_shapes=[
             pltpu.VMEM((tiles, width * chunk, 128), f32),
             pltpu.VMEM((tiles, heads * chunk, 128), f32),
-            pltpu.VMEM((per, tiles, residues, 128), f32),
+            pltpu.VMEM((tiles, n * heads * chunk, 128), f32),
             pltpu.VMEM((per, residues, residues), bf),
             pltpu.VMEM((rows, width, residues), bf),
             pltpu.VMEM((rows, width, residues), bf),
@@ -354,9 +363,9 @@
             dma((chunks, planes)), dma((chunks, planes, side)), dma((chunks, planes, side)), dma((chunks, n)),
         ],
         compiler_params=pltpu.CompilerParams(
-            collective_id=0, has_side_effects=True, vmem_limit_bytes=56 * 2**20
+            collective_id=0, has_side_effects=True, vmem_limit_bytes=60 * 2**20
         ),
-    )(pair, flat, flat, tri_in, tri_gate, tri_out, att_in, att_bias.T)
+    )(pair, turned, flat, tri_in, tri_gate, tri_out, att_in, att_bias.T)
 
     def whole(shape):
         return pl.BlockSpec(shape, lambda i: (0,) * len(shape))
@@ -365,22 +374,19 @@
         return pl.BlockSpec((1,) + shape, lambda i: (i, 0, 0))
 
     return pl.pallas_call(
-        functools.partial(attention_kernel, rows, heads),
+        functools.partial(attention_kernel, n),
         grid=(rows,),
         out_shape=jax.ShapeDtypeStruct((rows, residues, width), f32),
         in_specs=[
-            whole((chunks, n, heads * chunk, residues)), whole((1, residues)), smem,
+            whole((heads, residues, residues)), smem,
             row(width, residues), row(3 * hd, residues), row(hd, residues), whole((hd, width)),
         ],
         out_specs=row(residues, width),
         scratch_shapes=[
-            pltpu.VMEM((tiles, n * heads * chunk, 128), f32),
-            pltpu.VMEM((heads, tiles, residues, 128), f32),
-            pltpu.VMEM((heads, residues, residues), f32),
             pltpu.VMEM((width, hd), bf),
         ],
-        compiler_params=pltpu.CompilerParams(vmem_limit_bytes=48 * 2**20),
-    )(bias, flat, flat, pair1, qkv, gates, att_out)
+        compiler_params=pltpu.CompilerParams(vmem_limit_bytes=60 * 2**20),
+    )(bias, flat, pair1, qkv, gates, att_out)
 
 
 def layer_norm(value):
@@ -460,7 +466,7 @@
     def per_shard(pair, mask, tri_in, tri_gate, tri_out, att_in, att_bias, att_out):
         rows, residues, width = pair.shape
         fits = (
-            width % n == 0 and n % PLANE == 0 and n % 16 == 0 and residues % 128 == 0
+            rows * n == residues and width % n == 0 and n % PLANE == 0 and n % 16 == 0 and residues % 128 == 0
             and chunk_rows(n, rows, width, att_bias.shape[1]) > 0
         )
         run = functools.partial(fused, n) if fits else per_device

time: 143 us -> 141 us (0.986)
  local copies, waits for them, and re-layouts: 5.85 us -> 2.71 us
  Pallas kernels: 136 us -> 138 us
    unnamed x10 -> x0, local copies, waits for them, and re-layouts: 4.6 us -> none
    pallas_call x1, Pallas kernels: 112 us -> 113 us  [fused(): pl.pallas_call(functools.partial(triangle_kernel, n, chunk, heads), out_s...]
    reshape x0 -> x2, local copies, waits for them, and re-layouts: none -> 1.43 us  [fused(): turned = mask.reshape(n, rows).T.reshape(1, residues)]
where the time goes in v3:
time: 141 us
  Pallas kernels  138 us (98%)
  local copies, waits for them, and re-layouts  2.71 us (2%)
    pallas_call x1, Pallas kernels, fused(): pl.pallas_call(functools.partial(triangle_kernel, n, chunk, heads), out_s...  113 us
    pallas_call x1, Pallas kernels, fused(): pl.pallas_call(functools.partial(attention_kernel, n), grid=(rows,), out_...  24.6 us

profile of v3, /device:TPU:0, one launch (start us, length us, event | category | flops | bytes accessed | tf_op | source)
XLA Modules:
  0.0 140.7 jit_solution(5797967271905872755)
XLA Ops:
  0.0 1.2 reshape.11.live_ref
  1.2 0.8 reshape.9
  2.0 0.1 copy.9
  2.1 0.7 reshape.10.mask_ref
  2.7 113.4 %shard_map.82 = (f32[12,128,384]{2,1,0:T(8,128)}, bf16[12,384,384]{2,1,0:T(8,128)(2,1)}, f32[12,128,384]{2,1,0:T(8,128)}, f32[4,384,384]{2,1,0:T(8,128)}) custom-call(f32[12,384,128]{2,1,0:T(8,128)} %pair_ref.1, s32[1,384]{1,0:T(1,128)} %reshape.10.mask_ref, s32[1,384]{1,0:T(1,128)} %reshape.11.live_ref, bf16[128,512]{1,0:T(8,128)(2,1)} %tri_in_ref.1, ...), custom_call_target="tpu_custom_call" | custom-call | tf_op jit(solution)/shard_map/pallas_call | solution.py:338
  116.1 24.6 %shard_map.83 = f32[12,384,128]{2,1,0:T(8,128)} custom-call(f32[4,384,384]{2,1,0:T(8,128)} %get-tuple-element.9.bias_ref, s32[1,384]{1,0:T(1,128)} %reshape.11.live_ref, f32[12,128,384]{2,1,0:T(8,128)} %get-tuple-element.10.pair1_ref, bf16[12,384,384]{2,1,0:T(8,128)(2,1)} %get-tuple-element.11.qkv_ref, f32[12,128,384]{2,1,0:T(8,128)} %get-tuple-element.12.g_ref, ...), custom_call_target="tpu_custom_call" | custom-call | tf_op jit(solution)/shard_map/pallas_call | solution.py:376

commit v4 on v3

--- a/solution.py
+++ b/solution.py
@@ -47,14 +47,18 @@
 
 def triangle_kernel(
     n, chunk, heads,
-    pair_ref, mask_ref, live_ref, tri_in_ref, gate_ref, tri_out_ref, att_in_ref, bias_w_ref,
-    pair1_ref, qkv_ref, g_ref, bias_ref,
+    pair_hbm, mask_ref, tri_in_ref, gate_ref, tri_out_ref, att_in_ref, bias_w_ref,
+    pair1_hbm, qkv_hbm, g_hbm, bias_ref,
+    pair_ref, pair1_ref, qkv_ref, g_ref, pair_sem, out_sem,
     wide, bias_wide, bias_rows, right_mat, xn, yn, gating, tri_in_t, gate_t, tri_out_t, att_in_t,
     left_send, right_send, tri_send, left_got, right_got, tri_got, bias_all,
     left_ssem, left_rsem, right_ssem, right_rsem, tri_ssem, tri_rsem,
     z_ssem, plane_ssem, core_ssem, bias_rsem,
 ):
     rows, residues, width = pair_ref.shape
+    for u in range(rows // chunk):
+        at = pl.ds(u * chunk, chunk)
+        pltpu.make_async_copy(pair_hbm.at[at], pair_ref.at[at], pair_sem.at[u]).start()
     per = width // n
     block = per * chunk
     chunks = rows // chunk
@@ -112,10 +116,13 @@
     loop(1, n, lambda t: pl.semaphore_signal(
         barrier, inc=1, device_id=(group, lax.rem(me + t, n)), device_id_type=MESH))
 
-    valid = mask_ref[...].astype(jnp.float32)
+    length = lax.fori_loop(0, residues, lambda i, total: total + mask_ref[i], jnp.int32(0))
+    place = lax.broadcasted_iota(jnp.int32, (1, residues), 1)
+    natural = lax.rem(place, n) * rows + place // n
+    valid = jnp.where(natural < length, 1.0, 0.0)
 
     def pm(r):
-        return valid * live_ref[0, me * rows + r].astype(jnp.float32)
+        return valid * mask_ref[me * rows + r].astype(jnp.float32)
 
     tri_in_t[...] = to_t(tri_in_ref)
 
@@ -125,6 +132,9 @@
         scatter_rows(wide, place, chunk, value)
 
     for u in range(chunks):
+        at = pl.ds(u * chunk, chunk)
+        pltpu.make_async_copy(pair_hbm.at[at], pair_ref.at[at], pair_sem.at[u]).wait()
+
         def right_row(t):
             r = u * chunk + t
             pair_t = jnp.concatenate(
@@ -209,7 +219,7 @@
                 b = lax.rem(base + lax.rem(twin_low + 2 * step, PLANE) + z * PLANE, n)
                 put(u, b, core_ssem.at[u, z, step], me).wait_recv()
 
-    hide = jnp.where(mask_ref[...] > 0, 0.0, -jnp.inf)
+    hide = jnp.where(natural < length, 0.0, -jnp.inf)
 
     def bias_finish(u):
         bias_last(u)
@@ -241,6 +251,11 @@
         qkv_ref[r, :hd, :] = (qkvg[:hd] * scale).astype(jnp.bfloat16)
         qkv_ref[r, hd:, :] = qkvg[hd : 3 * hd].astype(jnp.bfloat16)
         g_ref[r] = sigmoid(qkvg[3 * hd :])
+
+    def store(u):
+        at = pl.ds(u * chunk, chunk)
+        pairs = ((pair1_ref, pair1_hbm), (qkv_ref, qkv_hbm), (g_ref, g_hbm))
+        return [pltpu.make_async_copy(v.at[at], h.at[at], out_sem.at[u, k]) for k, (v, h) in enumerate(pairs)]
 
     for u in range(chunks):
         receive_chunk(back, u)
@@ -258,6 +273,8 @@
         bias_first(u)
         if u < chunks - 1:
             loop(u * chunk, (u + 1) * chunk, qkvg_row)
+            for copy in store(u):
+                copy.start()
         if u >= 1:
             bias_second(u - 1)
         if u >= 2:
@@ -272,10 +289,14 @@
         bias_third(chunks - 2)
     bias_third(chunks - 1)
     loop(done + half, done + chunk, qkvg_row)
+    for copy in store(chunks - 1):
+        copy.start()
     for u in range(max(chunks - 2, 0), chunks):
         bias_finish(u)
     for u in range(chunks):
         bias_sent(u)
+        for copy in store(u):
+            copy.wait()
         for plan in (right, left, back):
             loop(1, n, lambda t: outgoing(plan, u, lax.rem(me + t, n)).wait_send())
 
@@ -291,23 +312,24 @@
         out_t[...] = to_t(att_out_ref)
 
     ones = jnp.ones((16, residues), jnp.bfloat16)
-    parts = []
-    for h in range(heads):
-        first = h * size
-        query = qkv_ref[0, first : first + size, :]
-        keys = qkv_ref[0, hd + first : hd + first + size, :]
-        values = qkv_ref[0, 2 * hd + first : 2 * hd + first + size, :]
-        scores = lax.dot_general(keys, query, (((0,), (0,)), ((), ())), preferred_element_type=jnp.float32)
-        scores = scores + bias_ref[h]
-        probs = jnp.exp2(scores - jnp.max(scores, axis=0, keepdims=True)).astype(jnp.bfloat16)
-        mixed = matmul(jnp.concatenate([values, ones], axis=0), probs)
-        gates = g_ref[0, first : first + size, :]
-        parts.append((mixed[:size] * (1.0 / mixed[size : size + 1]) * gates).astype(jnp.bfloat16))
-    out = matmul(out_t[...], jnp.concatenate(parts, axis=0))
-    live = live_ref[0, lax.axis_index("row") * rows + pl.program_id(0)].astype(jnp.float32)
-    new = (pair1_ref[0] + live * out).T
-    for r in range(rows):
-        out_ref[0, pl.ds(r, n, stride=rows), :] = new[r * n : (r + 1) * n]
+    for i in range(out_ref.shape[0]):
+        parts = []
+        for h in range(heads):
+            first = h * size
+            query = qkv_ref[i, first : first + size, :]
+            values = qkv_ref[i, 2 * hd + first : 2 * hd + first + size, :]
+            keys = qkv_ref[i, hd + first : hd + first + size, :]
+            scores = lax.dot_general(keys, query, (((0,), (0,)), ((), ())), preferred_element_type=jnp.float32)
+            scores = scores + bias_ref[h]
+            probs = jnp.exp2(scores - jnp.max(scores, axis=0, keepdims=True)).astype(jnp.bfloat16)
+            mixed = matmul(jnp.concatenate([values, ones], axis=0), probs)
+            gates = g_ref[i, first : first + size, :]
+            parts.append((mixed[:size] * (1.0 / mixed[size : size + 1]) * gates).astype(jnp.bfloat16))
+        out = matmul(out_t[...], jnp.concatenate(parts, axis=0))
+        own = lax.axis_index("row") * rows + pl.program_id(0) * out_ref.shape[0] + i
+        new = (pair1_ref[i] + live_ref[own].astype(jnp.float32) * out).T
+        for r in range(rows):
+            out_ref[i, pl.ds(r, n, stride=rows), :] = new[r * n : (r + 1) * n]
 
 
 def chunk_rows(n, rows, width, heads):
@@ -327,14 +349,14 @@
     chunks = rows // chunk
     tiles = residues // 128
     planes = n // PLANE
-    flat = mask.reshape(1, residues)
-    turned = mask.reshape(n, rows).T.reshape(1, residues)
     bf, f32 = jnp.bfloat16, jnp.float32
     vmem = pl.BlockSpec(memory_space=pltpu.VMEM)
     smem = pl.BlockSpec(memory_space=pltpu.SMEM)
+    hbm = pl.BlockSpec(memory_space=pl.ANY)
     dma = pltpu.SemaphoreType.DMA
     blocks = pltpu.VMEM((chunks, n, per * chunk, residues), bf)
     side = PLANE // 2
+    many = 3 if rows % 3 == 0 else 1
     pair1, qkv, gates, bias = pl.pallas_call(
         functools.partial(triangle_kernel, n, chunk, heads),
         out_shape=(
@@ -343,9 +365,15 @@
             jax.ShapeDtypeStruct((rows, hd, residues), f32),
             jax.ShapeDtypeStruct((heads, residues, residues), f32),
         ),
-        in_specs=[vmem, vmem, smem] + [vmem] * 5,
-        out_specs=(vmem,) * 4,
+        in_specs=[hbm, smem] + [vmem] * 5,
+        out_specs=(hbm, hbm, hbm, vmem),
         scratch_shapes=[
+            pltpu.VMEM((rows, residues, width), f32),
+            pltpu.VMEM((rows, width, residues), f32),
+            pltpu.VMEM((rows, 3 * hd, residues), bf),
+            pltpu.VMEM((rows, hd, residues), f32),
+            dma((chunks,)),
+            dma((chunks, 3)),
             pltpu.VMEM((tiles, width * chunk, 128), f32),
             pltpu.VMEM((tiles, heads * chunk, 128), f32),
             pltpu.VMEM((tiles, n * heads * chunk, 128), f32),
@@ -365,17 +393,17 @@
         compiler_params=pltpu.CompilerParams(
             collective_id=0, has_side_effects=True, vmem_limit_bytes=60 * 2**20
         ),
-    )(pair, turned, flat, tri_in, tri_gate, tri_out, att_in, att_bias.T)
+    )(pair, mask, tri_in, tri_gate, tri_out, att_in, att_bias.T)
 
     def whole(shape):
         return pl.BlockSpec(shape, lambda i: (0,) * len(shape))
 
     def row(*shape):
-        return pl.BlockSpec((1,) + shape, lambda i: (i, 0, 0))
+        return pl.BlockSpec((many,) + shape, lambda i: (i, 0, 0))
 
     return pl.pallas_call(
         functools.partial(attention_kernel, n),
-        grid=(rows,),
+        grid=(rows // many,),
         out_shape=jax.ShapeDtypeStruct((rows, residues, width), f32),
         in_specs=[
             whole((heads, residues, residues)), smem,
@@ -386,7 +414,7 @@
             pltpu.VMEM((width, hd), bf),
         ],
         compiler_params=pltpu.CompilerParams(vmem_limit_bytes=60 * 2**20),
-    )(bias, flat, pair1, qkv, gates, att_out)
+    )(bias, mask, pair1, qkv, gates, att_out)
 
 
 def layer_norm(value):

time: 141 us -> 135 us (0.957)
  Pallas kernels: 138 us -> 135 us
  local copies, waits for them, and re-layouts: 2.71 us -> 0 us
    reshape x3 -> x0, local copies, waits for them, and re-layouts: 2.63 us -> none  [the longest x2 1.43 us: fused(): turned = mask.reshape(n, rows).T.reshape(1, residues)]
    pallas_call x1, Pallas kernels: 113 us -> 112 us  [fused(): pl.pallas_call(functools.partial(triangle_kernel, n, chunk, heads), out_s...]
    pallas_call x1, Pallas kernels: 24.6 us -> 23.2 us  [fused(): pl.pallas_call(functools.partial(attention_kernel, n), grid=(rows // many...]
where the time goes in v4:
time: 135 us
  Pallas kernels  135 us (100%)
    pallas_call x1, Pallas kernels, fused(): pl.pallas_call(functools.partial(triangle_kernel, n, chunk, heads), out_s...  112 us
    pallas_call x1, Pallas kernels, fused(): pl.pallas_call(functools.partial(attention_kernel, n), grid=(rows // many...  23.2 us

profile of v4, /device:TPU:0, one launch (start us, length us, event | category | flops | bytes accessed | tf_op | source)
XLA Modules:
  0.0 135.0 jit_solution(4723580887539154425)
XLA Ops:
  0.0 111.9 %shard_map.82 = (f32[12,128,384]{2,1,0:T(8,128)}, bf16[12,384,384]{2,1,0:T(8,128)(2,1)}, f32[12,128,384]{2,1,0:T(8,128)}, f32[4,384,384]{2,1,0:T(8,128)}) custom-call(f32[12,384,128]{2,1,0:T(8,128)} %pair_hbm.1, s32[384]{0:T(512)} %live_ref.1, bf16[128,512]{1,0:T(8,128)(2,1)} %tri_in_ref.1, bf16[128,128]{1,0:T(8,128)(2,1)} %gate_ref.1, ...), custom_call_target="tpu_custom_call" | custom-call | tf_op jit(solution)/shard_map/pallas_call | solution.py:360
  111.9 23.2 %shard_map.83 = f32[12,384,128]{2,1,0:T(8,128)} custom-call(f32[4,384,384]{2,1,0:T(8,128)} %get-tuple-element.9.bias_ref, s32[384]{0:T(512)} %live_ref.1, f32[12,128,384]{2,1,0:T(8,128)} %get-tuple-element.10.pair1_ref, bf16[12,384,384]{2,1,0:T(8,128)(2,1)} %get-tuple-element.11.qkv_ref, f32[12,128,384]{2,1,0:T(8,128)} %get-tuple-element.12.g_ref, ...), custom_call_target="tpu_custom_call" | custom-call | tf_op jit(solution)/shard_map/pallas_call | solution.py:404

commit v5 on v4

--- a/solution.py
+++ b/solution.py
@@ -250,7 +250,7 @@
         qkvg = matmul(att_in_t[...], yn[r])
         qkv_ref[r, :hd, :] = (qkvg[:hd] * scale).astype(jnp.bfloat16)
         qkv_ref[r, hd:, :] = qkvg[hd : 3 * hd].astype(jnp.bfloat16)
-        g_ref[r] = sigmoid(qkvg[3 * hd :])
+        g_ref[r] = sigmoid(qkvg[3 * hd :]).astype(jnp.bfloat16)
 
     def store(u):
         at = pl.ds(u * chunk, chunk)
@@ -323,7 +323,7 @@
             scores = scores + bias_ref[h]
             probs = jnp.exp2(scores - jnp.max(scores, axis=0, keepdims=True)).astype(jnp.bfloat16)
             mixed = matmul(jnp.concatenate([values, ones], axis=0), probs)
-            gates = g_ref[i, first : first + size, :]
+            gates = g_ref[i, first : first + size, :].astype(jnp.float32)
             parts.append((mixed[:size] * (1.0 / mixed[size : size + 1]) * gates).astype(jnp.bfloat16))
         out = matmul(out_t[...], jnp.concatenate(parts, axis=0))
         own = lax.axis_index("row") * rows + pl.program_id(0) * out_ref.shape[0] + i
@@ -362,7 +362,7 @@
         out_shape=(
             jax.ShapeDtypeStruct((rows, width, residues), f32),
             jax.ShapeDtypeStruct((rows, 3 * hd, residues), bf),
-            jax.ShapeDtypeStruct((rows, hd, residues), f32),
+            jax.ShapeDtypeStruct((rows, hd, residues), bf),
             jax.ShapeDtypeStruct((heads, residues, residues), f32),
         ),
         in_specs=[hbm, smem] + [vmem] * 5,
@@ -371,7 +371,7 @@
             pltpu.VMEM((rows, residues, width), f32),
             pltpu.VMEM((rows, width, residues), f32),
             pltpu.VMEM((rows, 3 * hd, residues), bf),
-            pltpu.VMEM((rows, hd, residues), f32),
+            pltpu.VMEM((rows, hd, residues), bf),
             dma((chunks,)),
             dma((chunks, 3)),
             pltpu.VMEM((tiles, width * chunk, 128), f32),

time: 135 us -> 135 us (level)
  no operation moved by 1% of the time
where the time goes in v5:
time: 135 us
  Pallas kernels  135 us (100%)
    pallas_call x1, Pallas kernels, fused(): pl.pallas_call(functools.partial(triangle_kernel, n, chunk, heads), out_s...  112 us
    pallas_call x1, Pallas kernels, fused(): pl.pallas_call(functools.partial(attention_kernel, n), grid=(rows // many...  23.1 us

profile of v5, /device:TPU:0, one launch (start us, length us, event | category | flops | bytes accessed | tf_op | source)
XLA Modules:
  0.0 134.9 jit_solution(12634487161720345122)
XLA Ops:
  0.0 111.8 %shard_map.82 = (f32[12,128,384]{2,1,0:T(8,128)}, bf16[12,384,384]{2,1,0:T(8,128)(2,1)}, bf16[12,128,384]{2,1,0:T(8,128)(2,1)}, f32[4,384,384]{2,1,0:T(8,128)}) custom-call(f32[12,384,128]{2,1,0:T(8,128)} %pair_hbm.1, s32[384]{0:T(512)} %live_ref.1, bf16[128,512]{1,0:T(8,128)(2,1)} %tri_in_ref.1, bf16[128,128]{1,0:T(8,128)(2,1)} %gate_ref.1, ...), custom_call_target="tpu_custom_call" | custom-call | tf_op jit(solution)/shard_map/pallas_call | solution.py:360
  111.8 23.1 %shard_map.83 = f32[12,384,128]{2,1,0:T(8,128)} custom-call(f32[4,384,384]{2,1,0:T(8,128)} %get-tuple-element.9.bias_ref, s32[384]{0:T(512)} %live_ref.1, f32[12,128,384]{2,1,0:T(8,128)} %get-tuple-element.10.pair1_ref, bf16[12,384,384]{2,1,0:T(8,128)(2,1)} %get-tuple-element.11.qkv_ref, bf16[12,128,384]{2,1,0:T(8,128)(2,1)} %get-tuple-element.12.g_ref, ...), custom_call_target="tpu_custom_call" | custom-call | tf_op jit(solution)/shard_map/pallas_call | solution.py:404
